TPU v7x, 32 devices: a whole 2x2x4 slice. The times are simulated.
32 devices in a mesh: grp: 2 (over y), sec: 8 (over z, core), mpo: 2 (over x), sub: 1.
Axes of the slice: x: 2, y: 2, z: 4, core: 2. Of those that a mesh axis runs over, the one named last changes fastest.
Arguments:
- psi: bfloat16 [48, 512, 512], P(('grp', 'sec')), parts along dimension 0, may hold values from -6 to 6
- left_env: bfloat16 [14, 48, 512, 512], P('mpo', ('grp', 'sec')), parts along dimension 1, may hold values from -0.0625 to 0.0625
- right_env: bfloat16 [14, 48, 512, 512], P('mpo', ('grp', 'sec'), None, 'sub'), parts along dimension 1, may hold values from -0.25 to 0.25
- targets: int32 [24, 14], P('sec', 'mpo'), may hold values from 0 to 23, as said below
Outputs:
- sigma: bfloat16 [48, 512, 512], P(('grp', 'sec'), None, 'sub'), parts along dimension 0
There are 2 independent parts, one for each index of `grp`. A program takes and returns all parts, laid end to end along the dimension named above; an argument that names none is the same for every part. Nothing has to cross between parts.
Inputs may be any that keep to these rules, and one draw needn't show every extreme that they name: Among the entries of one device's block (one index of sec and one of mpo, 3 x 7 entries), at most 3 have targets // 3 equal to any one index of sec, and exactly 3 for some index.
All inputs are finite; a program needn't handle non-finite values.
Results may differ from a plain program's by a relative error of at most 0.0058.
Values may be sent and summed in bfloat16 or wider, within the bound.
A program may use at most 128 MiB of HBM per device.

v0:
```python
import jax
import jax.numpy as jnp
from jax import lax
from jax.sharding import PartitionSpec as P


def place_blocks(placing, contrib):
    return jnp.einsum(
        "sr,rac->sac", placing.astype(jnp.bfloat16), contrib, preferred_element_type=jnp.float32
    ).astype(jnp.bfloat16)


def local(psi, left_env, right_env, targets):
    sec_count = lax.axis_size("sec")
    sec_dev = psi.shape[0]
    width = psi.shape[1]
    terms_dev = left_env.shape[0]
    row_count = sec_dev * terms_dev
    capacity = max(2, (row_count + sec_count - 1) // sec_count)
    slot_count = sec_count * capacity
    inner = jnp.einsum("jab,wjbc->wjac", psi, right_env, preferred_element_type=jnp.float32).astype(
        jnp.bfloat16
    )
    contrib = jnp.einsum(
        "wjab,wjbc->jwac", left_env, inner, preferred_element_type=jnp.float32
    ).astype(jnp.bfloat16)
    half_width = contrib.shape[-1]
    contrib = contrib.reshape(row_count, width, half_width)
    flat_targets = targets.reshape(row_count)
    owner = flat_targets // sec_dev
    within = flat_targets % sec_dev
    same_owner = owner[:, None] == owner[None, :]
    row_order = jnp.arange(row_count)
    earlier = row_order[None, :] < row_order[:, None]
    rank = jnp.sum((same_owner & earlier).astype(jnp.int32), axis=1)
    slot = owner * capacity + rank
    placing = jnp.arange(slot_count)[:, None] == slot[None, :]
    labels = jnp.sum(jnp.where(placing, (within + 1)[None, :], 0), axis=1).astype(jnp.bfloat16)
    sector_marks = (jnp.arange(sec_dev) + 1).astype(jnp.bfloat16)
    outgoing = place_blocks(placing, contrib)
    incoming, arrived = (
        lax.all_to_all(outgoing, "sec", split_axis=0, concat_axis=0, tiled=True),
        lax.all_to_all(labels, "sec", split_axis=0, concat_axis=0, tiled=True),
    )
    collect = (arrived[None, :] == sector_marks[:, None]).astype(jnp.bfloat16)
    partial_value = jnp.einsum("ks,sac->kac", collect, incoming, preferred_element_type=jnp.float32)
    total = lax.psum(partial_value, "mpo")
    return total.astype(jnp.bfloat16)


def solution(mesh):
    placed = (
        P(("grp", "sec"), None, None),
        P("mpo", ("grp", "sec"), None, None),
        P("mpo", ("grp", "sec"), None, "sub"),
        P("sec", "mpo"),
    )
    return jax.shard_map(
        local, mesh=mesh, in_specs=placed, out_specs=P(("grp", "sec"), None, "sub"), check_vma=False
    )
```

profile of v0, /device:TPU:0, one launch (start us, length us, event | category | flops | bytes accessed | tf_op | source)
XLA Modules:
  0.0 441.2 jit_solution(10240418752606606880)
XLA Ops:
  0.0 0.0 copy-start
  0.0 0.8 broadcast_remainder_fusion
  0.8 0.7 sign_compare_fusion
  1.5 0.1 div.21
  1.6 0.1 rem.33
  1.7 0.1 ne.54
  1.8 0.2 convert_reduce_fusion
  2.0 0.1 select_reduce_fusion
  2.1 0.7 convert_element_type.53
  2.8 6.3 %all-to-all-start = ((bf16[8,3,1]{1,2,0:T(2,128)(2,1)}), bf16[8,3,1]{1,2,0:T(2,128)(2,1)S(1)}, u32[]{:S(2)}, u32[]{:S(2)}) async-start(bf16[8,3,1]{1,2,0:T(2,128)(2,1)} %convert_element_type.53), calls=%async_computation | async-start | bytes 8192 | tf_op jit(solution)/shard_map/all_to_all | solution.py:43
  9.1 0.0 copy-done
  9.1 17.6 %fusion.12 = bf16[3,7,512,512]{3,2,1,0:T(8,128)(2,1)} fusion(bf16[7,3,512,512]{3,2,1,0:T(8,128)(2,1)} %param.5, bf16[7,3,512,512]{3,2,1,0:T(8,128)(2,1)} %param.6, bf16[3,512,512]{2,1,0:T(8,128)(2,1)S(1)} %copy-done), kind=kOutput, calls=%fused_computation.8 | convolution fusion | flops 11285299200 | bytes 34603008 | tf_op jit(solution)/shard_map/wjab,wjbc->jwac/dot_general | solution.py:24
  26.7 17.0 %copy.26 = bf16[21,512,512]{2,0,1:T(8,128)(2,1)} copy(bf16[21,512,512]{1,2,0:T(8,128)(2,1)} %bitcast.21) | data formatting | bytes 22020096 | tf_op jit(solution)/shard_map/reshape | solution.py:28
  43.7 12.4 %convolution_convert_fusion = bf16[24,512,512]{2,0,1:T(8,128)(2,1)} fusion(bf16[21,512,512]{2,0,1:T(8,128)(2,1)} %copy.26, s32[21]{0:T(128)S(1)} %multiply_add_fusion), kind=kOutput, calls=%fused_computation.9 | convolution fusion | flops 270533120 | bytes 23593044 | tf_op jit(solution)/shard_map/sr,rac->sac/dot_general | solution.py:8
  56.1 12.9 %copy.27 = bf16[24,512,512]{2,1,0:T(8,128)(2,1)} copy(bf16[24,512,512]{2,0,1:T(8,128)(2,1)} %convolution_convert_fusion) | data formatting | bytes 25165824 | tf_op jit(solution)/shard_map/convert_element_type | solution.py:10
  69.0 0.0 all-to-all-done
  69.0 5.6 %all-to-all-start.1 = ((bf16[24,512,512]{2,1,0:T(8,128)(2,1)}), bf16[24,512,512]{2,1,0:T(8,128)(2,1)}, u32[]{:S(2)}, u32[]{:S(2)}) async-start(bf16[24,512,512]{2,1,0:T(8,128)(2,1)} %copy.27), calls=%async_computation.1 | async-start | bytes 25165824 | tf_op jit(solution)/shard_map/all_to_all | solution.py:42
  74.6 0.0 copy-start.1
  74.6 0.1 eq.49
  74.7 273.6 %all-to-all-done.1 = bf16[24,512,512]{2,1,0:T(8,128)(2,1)} async-done(((bf16[24,512,512]{2,1,0:T(8,128)(2,1)}), bf16[24,512,512]{2,1,0:T(8,128)(2,1)}, u32[]{:S(2)}, u32[]{:S(2)}) %all-to-all-start.1) | async-done | bytes 12582944 | tf_op jit(solution)/shard_map/all_to_all | solution.py:42
  348.3 13.4 %fusion = f32[3,512,512]{2,0,1:T(4,128)S(1)} fusion(bf16[24,512,512]{2,1,0:T(8,128)(2,1)} %all-to-all-done.1, bf16[24]{0:T(256)(128)(2,1)S(1)} %eq.49, bf16[3]{0:T(256)(128)(2,1)S(1)} %add_convert_fusion), kind=kOutput, calls=%fused_computation | convolution fusion | flops 37748952 | bytes 15728694 | tf_op jit(solution)/shard_map/ks,sac->kac/dot_general | solution.py:46
  361.7 2.6 copy.29
  364.3 76.9 %all-reduce.1 = bf16[3,512,512]{2,1,0:T(8,128)(2,1)} all-reduce(f32[3,512,512]{2,1,0:T(8,128)} %copy.29), channel_id=1, replica_groups=mesh['grp'=2,'sec'=8,'mpo'=2,'sub'=1] {'mpo'}, use_global_device_ids=true, to_apply=%region_2.3 | all-reduce | flops 786432 | bytes 4718592 | tf_op jit(solution)/shard_map/psum | solution.py:47
  441.2 0.0 copy-done.1
  (5 shorter events, 0.1 us)
Async XLA Ops:
  0.0 9.1 %copy-start = (bf16[3,512,512]{2,1,0:T(8,128)(2,1)S(1)}, bf16[3,512,512]{2,1,0:T(8,128)(2,1)}, u32[]{:S(2)}) copy-start(bf16[3,512,512]{2,1,0:T(8,128)(2,1)} %param.4) | copy-start | bytes 4718596
  2.8 66.2 %all-to-all-start = ((bf16[8,3,1]{1,2,0:T(2,128)(2,1)}), bf16[8,3,1]{1,2,0:T(2,128)(2,1)S(1)}, u32[]{:S(2)}, u32[]{:S(2)}) async-start(bf16[8,3,1]{1,2,0:T(2,128)(2,1)} %convert_element_type.53), calls=%async_computation | async-start | bytes 8192 | tf_op jit(solution)/shard_map/all_to_all | solution.py:43
  69.0 279.3 %all-to-all-start.1 = ((bf16[24,512,512]{2,1,0:T(8,128)(2,1)}), bf16[24,512,512]{2,1,0:T(8,128)(2,1)}, u32[]{:S(2)}, u32[]{:S(2)}) async-start(bf16[24,512,512]{2,1,0:T(8,128)(2,1)} %copy.27), calls=%async_computation.1 | async-start | bytes 25165824 | tf_op jit(solution)/shard_map/all_to_all | solution.py:42
  74.6 366.6 %copy-start.1 = (bf16[3,512,512]{2,1,0:T(8,128)(2,1)S(1)}, bf16[3,512,512]{2,1,0:T(8,128)(2,1)}, u32[]{:S(2)}) copy-start(bf16[3,512,512]{2,1,0:T(8,128)(2,1)} %param.4) | copy-start | bytes 4718596
where the time goes:
time: 442 us; the launch traced here: 441 us
  waiting for transfers between devices  274 us (62%)
  blocking collectives  76.9 us (17%)
  matrix products  43.4 us (10%)
  local copies, waits for them, and re-layouts  33.5 us (8%)
  starting transfers between devices  11.9 us (3%)
    all_to_all x1, waiting for transfers between devices, local(): lax.all_to_all(outgoing, 'sec', split_axis=0, concat_axis=0, tiled=True)  274 us
    psum x1, blocking collectives, local(): total = lax.psum(partial_value, 'mpo')  76.9 us
    dot_general x1, matrix products, local(): jnp.einsum('wjab,wjbc->jwac', left_env, inner, preferred_element_type=jnp...  17.6 us
    reshape x1, local copies, waits for them, and re-layouts, local(): contrib = contrib.reshape(row_count, width, half_width)  17 us
    dot_general x1, matrix products, local(): jnp.einsum('ks,sac->kac', collect, incoming, preferred_element_type=jnp.f...  13.4 us
    convert_element_type x1, local copies, waits for them, and re-layouts, place_blocks(): return jnp.einsum('sr,rac->sac', placing.astype(jnp.bfloat16), contrib, p...  12.9 us
    dot_general x1, matrix products, place_blocks(): jnp.einsum('sr,rac->sac', placing.astype(jnp.bfloat16), contrib, preferre...  12.4 us
  transfers between devices with their start and end apart: 2, of which 1 were waited for; matrix products, arithmetic and copies ran while one was open for 14% of the time, Pallas kernels for 0%

commit v1 on v0

v1 whole, which is shorter than its diff:
```python
import jax
import jax.numpy as jnp
from jax import lax
from jax.sharding import PartitionSpec as P


def local(psi, left_env, right_env, targets):
    sec_count = lax.axis_size("sec")
    sec_dev = psi.shape[0]
    width = psi.shape[1]
    terms_dev = left_env.shape[0]
    row_count = sec_dev * terms_dev
    inner = jnp.einsum("jab,wjbc->wjac", psi, right_env, preferred_element_type=jnp.float32).astype(
        jnp.bfloat16
    )
    contrib = jnp.einsum(
        "wjab,wjbc->jwac", left_env, inner, preferred_element_type=jnp.float32
    ).astype(jnp.bfloat16)
    half_width = contrib.shape[-1]
    contrib = contrib.reshape(row_count, width, half_width)
    flat_targets = targets.reshape(row_count)
    placing = (jnp.arange(sec_count * sec_dev)[:, None] == flat_targets[None, :]).astype(jnp.bfloat16)
    partial = jnp.einsum(
        "kr,rac->kac", placing, contrib, preferred_element_type=jnp.float32
    ).astype(jnp.bfloat16)
    mine = lax.psum_scatter(partial, "sec", scatter_dimension=0, tiled=True)
    total = lax.psum(mine.astype(jnp.float32), "mpo")
    return total.astype(jnp.bfloat16)


def solution(mesh):
    placed = (
        P(("grp", "sec"), None, None),
        P("mpo", ("grp", "sec"), None, None),
        P("mpo", ("grp", "sec"), None, "sub"),
        P("sec", "mpo"),
    )
    return jax.shard_map(
        local, mesh=mesh, in_specs=placed, out_specs=P(("grp", "sec"), None, "sub"), check_vma=False
    )
```

time: 442 us -> 262 us (0.59)
  waiting for transfers between devices: 274 us -> 184 us
  blocking collectives: 76.9 us -> 0 us
  matrix products: 43.4 us -> 30 us
  between operations: 0.05 us -> 13.4 us
  starting transfers between devices: 11.9 us -> 0.04 us
    all_to_all x2 -> x0, waiting for transfers between devices: 274 us -> none  [the longest x1 274 us: local(): lax.all_to_all(outgoing, 'sec', split_axis=0, concat_axis=0, tiled=True)]
    reduce_scatter x0 -> x1, waiting for transfers between devices: none -> 132 us  [local(): mine = lax.psum_scatter(partial, 'sec', scatter_dimension=0, tiled=True)]
    psum x1 -> x0, blocking collectives: 76.9 us -> none  [local(): total = lax.psum(partial_value, 'mpo')]
    psum x0 -> x1, waiting for transfers between devices: none -> 52.1 us  [local(): total = lax.psum(mine.astype(jnp.float32), 'mpo')]
    dot_general x2 -> x1, matrix products: 25.9 us -> 12.5 us  [local(): jnp.einsum('kr,rac->kac', placing, contrib, preferred_element_type=jnp.fl...]
    all_to_all x2 -> x0, starting transfers between devices: 11.9 us -> none  [the longest x1 6.33 us: local(): lax.all_to_all(labels, 'sec', split_axis=0, concat_axis=0, tiled=True)]
    convert_element_type x2 -> x1, local copies, waits for them, and re-layouts: 13.6 us -> 13 us  [local(): partial = jnp.einsum('kr,rac->kac', placing, contrib, preferred_element_t...]
  transfers between devices with their start and end apart: 2 -> 2, of which waited for: 1 -> 2; matrix products, arithmetic and copies ran while one was open for 14% -> 0% of each run, Pallas kernels for 0% -> 0%
where the time goes in v1:
time: 262 us
  waiting for transfers between devices  184 us (70%)
  local copies, waits for them, and re-layouts  34.1 us (13%)
  matrix products  30 us (11%)
  between operations  13.4 us (5%)
    reduce_scatter x1, waiting for transfers between devices, local(): mine = lax.psum_scatter(partial, 'sec', scatter_dimension=0, tiled=True)  132 us
    psum x1, waiting for transfers between devices, local(): total = lax.psum(mine.astype(jnp.float32), 'mpo')  52.1 us
    dot_general x1, matrix products, local(): jnp.einsum('wjab,wjbc->jwac', left_env, inner, preferred_element_type=jnp...  17.6 us
    reshape x1, local copies, waits for them, and re-layouts, local(): contrib = contrib.reshape(row_count, width, half_width)  17 us
    convert_element_type x1, local copies, waits for them, and re-layouts, local(): partial = jnp.einsum('kr,rac->kac', placing, contrib, preferred_element_t...  13 us
    dot_general x1, matrix products, local(): jnp.einsum('kr,rac->kac', placing, contrib, preferred_element_type=jnp.fl...  12.5 us
  transfers between devices with their start and end apart: 2, of which 2 were waited for; matrix products, arithmetic and copies ran while one was open for 0% of the time, Pallas kernels for 0%

profile of v1, /device:TPU:0, one launch (start us, length us, event | category | flops | bytes accessed | tf_op | source)
XLA Modules:
  0.0 261.7 jit_solution(2623363130291045983)
XLA Ops:
  6.5 0.0 copy-start
  6.5 0.0 reduce-scatter.2.cloned.1.call-start
  6.5 0.9 eq.16
  7.4 0.5 copy-done
  8.0 17.6 %fusion.10 = bf16[3,7,512,512]{3,2,1,0:T(8,128)(2,1)} fusion(bf16[7,3,512,512]{3,2,1,0:T(8,128)(2,1)} %param.5, bf16[7,3,512,512]{3,2,1,0:T(8,128)(2,1)} %param.6, bf16[3,512,512]{2,1,0:T(8,128)(2,1)S(1)} %copy-done), kind=kOutput, calls=%fused_computation.6 | convolution fusion | flops 11285299200 | bytes 34603008 | tf_op jit(solution)/shard_map/wjab,wjbc->jwac/dot_general | solution.py:16
  25.5 17.0 %copy.9 = bf16[21,512,512]{2,0,1:T(8,128)(2,1)} copy(bf16[21,512,512]{1,2,0:T(8,128)(2,1)} %bitcast.18) | data formatting | bytes 22020096 | tf_op jit(solution)/shard_map/reshape | solution.py:20
  42.5 12.5 %convolution_convert_fusion = bf16[24,512,512]{2,0,1:T(8,128)(2,1)} fusion(bf16[21,512,512]{2,0,1:T(8,128)(2,1)} %copy.9, s32[21]{0:T(128)S(1)} %eq.16), kind=kOutput, calls=%fused_computation.7 | convolution fusion | flops 270533120 | bytes 23593044 | tf_op jit(solution)/shard_map/kr,rac->kac/dot_general | solution.py:23
  54.9 0.0 copy-start.1
  54.9 13.0 %copy.10 = bf16[24,512,512]{2,1,0:T(8,128)(2,1)} copy(bf16[24,512,512]{2,0,1:T(8,128)(2,1)} %convolution_convert_fusion) | data formatting | bytes 25165824 | tf_op jit(solution)/shard_map/convert_element_type | solution.py:25
  68.0 0.0 reduce-scatter.2.cloned.1.call-update
  68.0 0.0 all-reduce.2.cloned.1.call-start
  68.0 132.0 %reduce-scatter.2.cloned.1.call-done = bf16[3,512,512]{2,1,0:T(8,128)(2,1)} async-done(((bf16[24,512,512]{2,1,0:T(8,128)(2,1)}), bf16[3,512,512]{2,1,0:T(8,128)(2,1)}) %reduce-scatter.2.cloned.1.call-update) | async-done | bytes 1572880 | tf_op jit(solution)/shard_map/reduce_scatter | solution.py:26
  200.1 0.0 all-reduce.2.cloned.1.call-update
  200.1 52.1 %all-reduce.2.cloned.1.call-done = bf16[3,512,512]{2,1,0:T(8,128)(2,1)} async-done(((bf16[3,512,512]{2,1,0:T(8,128)(2,1)}), bf16[3,512,512]{2,1,0:T(8,128)(2,1)}) %all-reduce.2.cloned.1.call-update) | async-done | bytes 1572880 | tf_op jit(solution)/shard_map/psum | solution.py:27
  252.2 2.7 %copy.26 = bf16[3,512,512]{2,1,0:T(8,128)(2,1)} copy(bf16[3,512,512]{2,1,0:T(8,128)(2,1)} %all-reduce.2.cloned.1.call-done) | data formatting | bytes 3145728
  254.9 0.0 copy-done.1
Async XLA Ops:
  6.5 1.4 copy-start
  6.5 193.5 %reduce-scatter.2.cloned.1.call-start = ((), (), s32[]{:S(2)}) async-start(), calls=%async_computation.1 | async-start | bytes 14155776 | tf_op jit(solution)/shard_map/reduce_scatter | solution.py:26
  54.9 199.9 %copy-start.1 = (bf16[3,512,512]{2,1,0:T(8,128)(2,1)S(1)}, bf16[3,512,512]{2,1,0:T(8,128)(2,1)}, u32[]{:S(2)}) copy-start(bf16[3,512,512]{2,1,0:T(8,128)(2,1)} %param.4) | copy-start | bytes 4718596
  68.0 184.2 %all-reduce.2.cloned.1.call-start = ((), (), s32[]{:S(2)}) async-start(), calls=%async_computation.2 | async-start | bytes 3145728 | tf_op jit(solution)/shard_map/psum | solution.py:27
Sparse Core Ops, SparseCore 0:
  68.1 131.9 reduce-scatter.1
  202.4 49.8 all-reduce.1

commit v2 on v1

v2 whole, which is shorter than its diff:
```python
import functools

import jax
import jax.numpy as jnp
from jax import lax
from jax.experimental import pallas as pl
from jax.experimental.pallas import tpu as pltpu
from jax.sharding import PartitionSpec as P

MESH = pl.DeviceIdType.MESH
F32 = jnp.float32
BF16 = jnp.bfloat16


def first_rows(width, mpo):
    return max(16, (width * 2 // 3 // mpo + 8) // 16 * 16)


def kernel(
    n, cores, mpo, cap, hx,
    slots_ref, marks_ref, psi_hbm, left_hbm, right_hbm, out_ref,
    pv, lv, rv, sib_send, sib_recv, own_p, own_b, x_recv, z_p, z_b, fin_p, fin_b,
    in_sem, sib_ssem, sib_rsem, x_ssem, x_rsem, zp_ssem, zp_rsem, zb_ssem, zb_rsem,
    fp_ssem, fp_rsem, fb_ssem, fb_rsem,
):
    terms = lv.shape[0]
    sec_dev, width, cols = pv.shape[0], lv.shape[1], rv.shape[2]
    hb = width - mpo * hx
    sec = lax.axis_index("sec")
    me = lax.axis_index("mpo")
    z = lax.div(sec, cores)
    c = lax.rem(sec, cores)
    sibling = {"sec": z * cores + (1 - c)}
    right_dev = {"sec": sec + cores}
    left_dev = {"sec": sec - cores}

    def other(d):
        return lax.rem(me + d, mpo)

    def load_psi():
        return pltpu.make_async_copy(psi_hbm, pv, in_sem.at[2 * terms])

    def load_right(r):
        return pltpu.make_async_copy(right_hbm.at[r], rv.at[r], in_sem.at[r])

    def load_left(r):
        return pltpu.make_async_copy(left_hbm.at[r], lv.at[r], in_sem.at[terms + r])

    load_psi().start()

    @pl.loop(0, terms)
    def _(r):
        load_right(r).start()

    @pl.loop(0, terms)
    def _(r):
        load_left(r).start()

    barrier = pltpu.get_barrier_semaphore()
    if cores == 2:
        pl.semaphore_signal(barrier, inc=1, device_id=sibling, device_id_type=MESH)
    for d in range(1, mpo):
        pl.semaphore_signal(barrier, inc=1, device_id={"mpo": other(d)}, device_id_type=MESH)

    @pl.when(z > 0)
    def _():
        pl.semaphore_signal(barrier, inc=1, device_id=left_dev, device_id_type=MESH)

    @pl.when(z < n - 1)
    def _():
        pl.semaphore_signal(barrier, inc=1, device_id=right_dev, device_id_type=MESH)

    peers = cores - 1 + mpo - 1 + jnp.minimum(z, 1) + jnp.minimum(n - 1 - z, 1)
    pl.semaphore_wait(barrier, peers)

    def target(k):
        near_left = 2 * z <= n - 1
        lead = jnp.where(near_left, n - 1 - 2 * z, 2 * z - (n - 1))
        q = jnp.maximum(k - lead, 0)
        half = lax.div(q, 2)
        odd = lax.rem(q, 2) == 1
        ahead = jnp.minimum(k, lead)
        t_left = jnp.where(odd, half, n - 1 - ahead - half)
        t_right = jnp.where(odd, n - 1 - half, ahead + half)
        return jnp.where(near_left, t_left, t_right)

    def sib_copy(t):
        return pltpu.make_async_remote_copy(
            src_ref=sib_send.at[t], dst_ref=sib_recv.at[t],
            send_sem=sib_ssem.at[t], recv_sem=sib_rsem.at[t],
            device_id=sibling, device_id_type=MESH)

    def x_copy(t, s, d):
        return pltpu.make_async_remote_copy(
            src_ref=own_p.at[t, other(d), s], dst_ref=x_recv.at[mpo - d - 1, t, s],
            send_sem=x_ssem.at[d - 1, t, s], recv_sem=x_rsem.at[mpo - d - 1, t, s],
            device_id={"mpo": other(d)}, device_id_type=MESH)

    def x_wait(t, s, d):
        pltpu.make_async_remote_copy(
            src_ref=own_p.at[t, other(d), s], dst_ref=x_recv.at[d - 1, t, s],
            send_sem=x_ssem.at[d - 1, t, s], recv_sem=x_rsem.at[d - 1, t, s],
            device_id={"mpo": other(d)}, device_id_type=MESH).wait_recv()

    def zp_copy(t, s, slot, dev):
        return pltpu.make_async_remote_copy(
            src_ref=own_p.at[t, me, s], dst_ref=z_p.at[slot, s],
            send_sem=zp_ssem.at[t, s], recv_sem=zp_rsem.at[slot, s],
            device_id=dev, device_id_type=MESH)

    def zb_copy(t, s, slot, dev):
        return pltpu.make_async_remote_copy(
            src_ref=own_b.at[t, s], dst_ref=z_b.at[slot, s],
            send_sem=zb_ssem.at[t, s], recv_sem=zb_rsem.at[slot, s],
            device_id=dev, device_id_type=MESH)

    def z_send(copy, t, s):
        @pl.when(t > z)
        def _():
            copy(t, s, t, right_dev).start()

        @pl.when(t < z)
        def _():
            copy(t, s, jnp.where(t == z - 1, n, t), left_dev).start()

    def fp_copy(s, d):
        return pltpu.make_async_remote_copy(
            src_ref=fin_p.at[me, s], dst_ref=fin_p.at[me, s],
            send_sem=fp_ssem.at[d - 1, s], recv_sem=fp_rsem.at[me, s],
            device_id={"mpo": other(d)}, device_id_type=MESH)

    def fb_copy(s, d):
        return pltpu.make_async_remote_copy(
            src_ref=fin_b.at[me, s], dst_ref=fin_b.at[me, s],
            send_sem=fb_ssem.at[d - 1, s], recv_sem=fb_rsem.at[me, s],
            device_id={"mpo": other(d)}, device_id_type=MESH)

    def fp_wait(s, d):
        o = other(d)
        pltpu.make_async_remote_copy(
            src_ref=fin_p.at[o, s], dst_ref=fin_p.at[o, s],
            send_sem=fp_ssem.at[d - 1, s], recv_sem=fp_rsem.at[o, s],
            device_id={"mpo": o}, device_id_type=MESH).wait_recv()

    def fb_wait(s, d):
        o = other(d)
        pltpu.make_async_remote_copy(
            src_ref=fin_b.at[o, s], dst_ref=fin_b.at[o, s],
            send_sem=fb_ssem.at[d - 1, s], recv_sem=fb_rsem.at[o, s],
            device_id={"mpo": o}, device_id_type=MESH).wait_recv()

    load_psi().wait()
    col_tile = min(cols, 256)

    @pl.loop(0, terms)
    def _(r):
        load_right(r).wait()
        j = lax.rem(r, sec_dev)
        for c0 in range(0, cols, col_tile):
            rv[r, :, c0:c0 + col_tile] = jnp.dot(
                pv[j], rv[r, :, c0:c0 + col_tile], preferred_element_type=F32
            ).astype(BF16)

    @pl.loop(0, terms)
    def _(r):
        load_left(r).wait()

    def partial_rows(owner, row0, rows):
        products = []
        for i in range(cap):
            r = slots_ref[owner * cap + i]
            products.append(jnp.dot(lv[r, row0:row0 + rows, :], rv[r], preferred_element_type=F32))
        for s in range(sec_dev):
            total = None
            for i in range(cap):
                term = products[i] * marks_ref[(owner * cap + i) * sec_dev + s]
                total = term if total is None else total + term
            yield s, total.astype(BF16)

    parts = [(m * hx, hx, m) for m in range(mpo)] + [(mpo * hx, hb, None)]

    def make_sums(t):
        if cores == 2:
            for row0, rows, m in parts:
                for s, value in partial_rows(t * cores + (1 - c), row0, rows):
                    sib_send[t, s, row0:row0 + rows, :] = value
            sib_copy(t).start()
        for row0, rows, m in parts:
            for s, value in partial_rows(t * cores + c, row0, rows):
                if m is None:
                    own_b[t, s] = value
                else:
                    own_p[t, m, s] = value

    def add_sibling(t):
        if cores == 2:
            sib_copy(t).wait_recv()
        for s in range(sec_dev):
            if cores == 2:
                for m in range(mpo):
                    own_p[t, m, s] = (
                        own_p[t, m, s].astype(F32)
                        + sib_recv[t, s, m * hx:(m + 1) * hx, :].astype(F32)
                    ).astype(BF16)
                own_b[t, s] = (
                    own_b[t, s].astype(F32) + sib_recv[t, s, mpo * hx:, :].astype(F32)
                ).astype(BF16)
            for d in range(1, mpo):
                x_copy(t, s, d).start()

            @pl.when(z == 0)
            def _():
                @pl.when(t > 0)
                def _():
                    zb_copy(t, s, t, right_dev).start()

            @pl.when(z == n - 1)
            def _():
                @pl.when(t < n - 1)
                def _():
                    zb_copy(t, s, jnp.where(t == z - 1, n, t), left_dev).start()

    @pl.loop(0, n)
    def _(k):
        make_sums(target(k))

        @pl.when(k > 0)
        def _():
            add_sibling(target(k - 1))

    add_sibling(z)

    def add_to(ref, values):
        total = ref[...].astype(F32)
        for v in values:
            total = total + v.astype(F32)
        ref[...] = total.astype(BF16)

    @pl.loop(0, n - 1)
    def _(k):
        t = target(k)
        inside = jnp.logical_or(jnp.logical_and(t > z, z > 0), jnp.logical_and(t < z, z < n - 1))

        @pl.loop(0, sec_dev)
        def _(s):
            @pl.when(inside)
            def _():
                zb_copy(t, s, t, right_dev).wait_recv()
                add_to(own_b.at[t, s], [z_b[t, s]])
                z_send(zb_copy, t, s)

            for d in range(1, mpo):
                x_wait(t, s, d)

            @pl.when(inside)
            def _():
                zp_copy(t, s, t, right_dev).wait_recv()
                add_to(own_p.at[t, me, s], [x_recv[d, t, s] for d in range(mpo - 1)] + [z_p[t, s]])

            @pl.when(jnp.logical_not(inside))
            def _():
                add_to(own_p.at[t, me, s], [x_recv[d, t, s] for d in range(mpo - 1)])

            z_send(zp_copy, t, s)

    @pl.loop(0, sec_dev)
    def _(s):
        @pl.when(z > 0)
        def _():
            zb_copy(z, s, z, left_dev).wait_recv()
            add_to(own_b.at[z, s], [z_b[z, s]])

        @pl.when(z < n - 1)
        def _():
            zb_copy(z, s, n, right_dev).wait_recv()
            add_to(own_b.at[z, s], [z_b[n, s]])

        fin_b[me, s] = own_b[z, s]
        for d in range(1, mpo):
            fb_copy(s, d).start()
            x_wait(z, s, d)
        add_to(own_p.at[z, me, s], [x_recv[d, z, s] for d in range(mpo - 1)])

        @pl.when(z > 0)
        def _():
            zp_copy(z, s, z, left_dev).wait_recv()
            add_to(own_p.at[z, me, s], [z_p[z, s]])

        @pl.when(z < n - 1)
        def _():
            zp_copy(z, s, n, right_dev).wait_recv()
            add_to(own_p.at[z, me, s], [z_p[n, s]])

        fin_p[me, s] = own_p[z, me, s]
        for d in range(1, mpo):
            fp_copy(s, d).start()

    @pl.loop(0, sec_dev)
    def _(s):
        for d in range(1, mpo):
            fb_wait(s, d)
        total = fin_b[0, s].astype(F32)
        for m in range(1, mpo):
            total = total + fin_b[m, s].astype(F32)
        out_ref[s, mpo * hx:, :] = total.astype(BF16)
        for d in range(1, mpo):
            fp_wait(s, d)
        for m in range(mpo):
            out_ref[s, m * hx:(m + 1) * hx, :] = fin_p[m, s]

    @pl.loop(0, n)
    def _(t):
        if cores == 2:
            sib_copy(t).wait_send()

        @pl.loop(0, sec_dev)
        def _(s):
            for d in range(1, mpo):
                x_copy(t, s, d).wait_send()

            @pl.when(t != z)
            def _():
                zp_copy(t, s, t, right_dev).wait_send()
                zb_copy(t, s, t, right_dev).wait_send()

    @pl.loop(0, sec_dev)
    def _(s):
        for d in range(1, mpo):
            fp_copy(s, d).wait_send()
            fb_copy(s, d).wait_send()


def local(mesh, psi, left_env, right_env, targets):
    sec_count, mpo = mesh.shape["sec"], mesh.shape["mpo"]
    cores = 2 if mesh.shape["sub"] == 1 and sec_count % 2 == 0 else 1
    n = sec_count // cores
    sec_dev, width = psi.shape[:2]
    terms = left_env.shape[0] * sec_dev
    cols = right_env.shape[-1]
    cap = max(2, -(-terms // sec_count))
    hx = first_rows(width, mpo)
    hb = width - mpo * hx
    flat = targets.T.reshape(terms)
    owner, within = flat // sec_dev, flat % sec_dev
    rows = jnp.arange(terms)
    earlier = (owner[:, None] == owner[None, :]) & (rows[None, :] < rows[:, None])
    slot = owner * cap + jnp.sum(earlier.astype(jnp.int32), axis=1)
    placing = jnp.arange(sec_count * cap)[:, None] == slot[None, :]
    slots = jnp.sum(jnp.where(placing, rows[None, :], 0), axis=1).astype(jnp.int32)
    marks = jnp.any(
        placing[:, None, :] & (within[None, None, :] == jnp.arange(sec_dev)[None, :, None]), axis=2
    ).astype(F32).reshape(-1)

    vm = lambda *shape: pltpu.VMEM(shape, BF16)
    sem = lambda *shape: pltpu.SemaphoreType.DMA(shape)
    sib = (n, sec_dev, width, cols) if cores == 2 else (1, 1, 16, 128)
    xs = max(mpo - 1, 1)
    return pl.pallas_call(
        functools.partial(kernel, n, cores, mpo, cap, hx),
        out_shape=jax.ShapeDtypeStruct((sec_dev, width, cols), BF16),
        in_specs=[pl.BlockSpec(memory_space=pltpu.SMEM)] * 2 + [pl.BlockSpec(memory_space=pl.ANY)] * 3,
        out_specs=pl.BlockSpec(memory_space=pltpu.VMEM),
        scratch_shapes=[
            vm(sec_dev, width, width), vm(terms, width, width), vm(terms, width, cols),
            vm(*sib), vm(*sib),
            vm(n, mpo, sec_dev, hx, cols), vm(n, sec_dev, hb, cols),
            vm(xs, n, sec_dev, hx, cols),
            vm(n + 1, sec_dev, hx, cols), vm(n + 1, sec_dev, hb, cols),
            vm(mpo, sec_dev, hx, cols), vm(mpo, sec_dev, hb, cols),
            sem(2 * terms + 1), sem(n), sem(n),
            sem(xs, n, sec_dev), sem(xs, n, sec_dev),
            sem(n, sec_dev), sem(n + 1, sec_dev), sem(n, sec_dev), sem(n + 1, sec_dev),
            sem(xs, sec_dev), sem(mpo, sec_dev), sem(xs, sec_dev), sem(mpo, sec_dev),
        ],
        compiler_params=pltpu.CompilerParams(
            collective_id=0, has_side_effects=True, vmem_limit_bytes=60 * 1024 * 1024
        ),
        cost_estimate=pl.CostEstimate(
            flops=4 * terms * width * width * cols,
            bytes_accessed=2 * terms * width * (width + cols), transcendentals=0,
        ),
    )(
        slots, marks, psi, left_env.reshape(terms, width, width), right_env.reshape(terms, width, cols)
    )


def solution(mesh):
    placed = (
        P(("grp", "sec"), None, None),
        P("mpo", ("grp", "sec"), None, None),
        P("mpo", ("grp", "sec"), None, "sub"),
        P("sec", "mpo"),
    )
    return jax.shard_map(
        functools.partial(local, mesh), mesh=mesh, in_specs=placed,
        out_specs=P(("grp", "sec"), None, "sub"), check_vma=False,
    )
```

time: 262 us -> 113 us (0.43)
  waiting for transfers between devices: 184 us -> 0 us
  Pallas kernels: 0 us -> 107 us
  local copies, waits for them, and re-layouts: 34.1 us -> 3.93 us
  matrix products: 30 us -> 0 us
  between operations: 13.4 us -> 0.02 us
    reduce_scatter x1 -> x0, waiting for transfers between devices: 132 us -> none  [local(): mine = lax.psum_scatter(partial, 'sec', scatter_dimension=0, tiled=True)]
    pallas_call x0 -> x1, Pallas kernels: none -> 107 us  [local(): pl.pallas_call(functools.partial(kernel, n, cores, mpo, cap, hx), out_sha...]
    psum x1 -> x0, waiting for transfers between devices: 52.1 us -> none  [local(): total = lax.psum(mine.astype(jnp.float32), 'mpo')]
    dot_general x2 -> x0, matrix products: 30 us -> none  [the longest x1 17.6 us: local(): jnp.einsum('wjab,wjbc->jwac', left_env, inner, preferred_element_type=jnp...]
    reshape x1 -> x0, local copies, waits for them, and re-layouts: 17 us -> none  [local(): contrib = contrib.reshape(row_count, width, half_width)]
    convert_element_type x1 -> x2, local copies, waits for them, and re-layouts: 13 us -> 0.73 us  [local(): marks = jnp.any(placing[:, None, :] & (within[None, None, :] == jnp.arang...]
  transfers between devices with their start and end apart: 2 -> 0, of which waited for: 2 -> 0; matrix products, arithmetic and copies ran while one was open for 0% -> 0% of each run, Pallas kernels for 0% -> 0%
where the time goes in v2:
time: 113 us
  Pallas kernels  107 us (95%)
  local copies, waits for them, and re-layouts  3.93 us (3%)
  other arithmetic  2.38 us (2%)
    pallas_call x1, Pallas kernels, local(): pl.pallas_call(functools.partial(kernel, n, cores, mpo, cap, hx), out_sha...  107 us
    unnamed x1, local copies, waits for them, and re-layouts  2.65 us

profile of v2, /device:TPU:0, one launch (start us, length us, event | category | flops | bytes accessed | tf_op | source)
XLA Modules:
  0.0 112.9 jit_solution(13951181290646771613)
XLA Ops:
  0.0 0.7 fusion.1
  0.7 0.1 copy.11
  0.8 0.1 ne.57
  0.9 0.7 remainder_bitcast_fusion
  1.6 0.1 copy.12
  1.7 0.1 rem.38
  1.8 0.1 copy.13
  1.9 0.1 div.25
  2.0 0.2 convert_reduce_fusion
  2.1 0.6 select_reduce_fusion.slots_ref
  2.8 0.2 and_reduce_fusion
  2.9 0.1 copy.14
  3.0 0.6 reshape.118.marks_ref
  3.7 106.5 %shard_map.46 = bf16[3,512,512]{2,1,0:T(8,128)(2,1)} custom-call(s32[24]{0:T(128)} %select_reduce_fusion.slots_ref, f32[72]{0:T(128)} %reshape.118.marks_ref, bf16[3,512,512]{2,1,0:T(8,128)(2,1)} %psi_hbm.1, bf16[21,512,512]{2,1,0:T(8,128)(2,1)} %bitcast.8, bf16[21,512,512]{2,1,0:T(8,128)(2,1)} %bitcast.9), custom_call_target="tpu_custom_call" | custom-call | flops 11274289152 | bytes 22020096 | tf_op jit(solution)/shard_map/pallas_call | solution.py:358
  110.2 2.7 %copy.16 = bf16[3,512,512]{2,1,0:T(8,128)(2,1)} copy(bf16[3,512,512]{2,1,0:T(8,128)(2,1)} %shard_map.46) | data formatting | bytes 3145728
  (5 shorter events, 0.0 us)

commit v3 on v2

--- a/solution.py
+++ b/solution.py
@@ -18,8 +18,8 @@
 
 def kernel(
     n, cores, mpo, cap, hx,
-    slots_ref, marks_ref, psi_hbm, left_hbm, right_hbm, out_ref,
-    pv, lv, rv, sib_send, sib_recv, own_p, own_b, x_recv, z_p, z_b, fin_p, fin_b,
+    targets_ref, psi_hbm, left_hbm, right_hbm, out_ref,
+    slots_ref, marks_ref, pv, lv, rv, sib_send, sib_recv, own_p, own_b, x_recv, z_p, z_b, fin_p, fin_b,
     in_sem, sib_ssem, sib_rsem, x_ssem, x_rsem, zp_ssem, zp_rsem, zb_ssem, zb_rsem,
     fp_ssem, fp_rsem, fb_ssem, fb_rsem,
 ):
@@ -70,6 +70,26 @@
     def _():
         pl.semaphore_signal(barrier, inc=1, device_id=right_dev, device_id_type=MESH)
 
+    goals = [targets_ref[r % sec_dev, r // sec_dev] for r in range(terms)]
+
+    @pl.loop(0, n * cores)
+    def _(owner):
+        low = owner * sec_dev
+        count = jnp.int32(0)
+        row = [jnp.int32(0)] * cap
+        goal = [jnp.int32(-1)] * cap
+        for r in range(terms):
+            hit = jnp.logical_and(goals[r] >= low, goals[r] < low + sec_dev)
+            for i in range(cap):
+                take = jnp.logical_and(hit, count == i)
+                row[i] = jnp.where(take, r, row[i])
+                goal[i] = jnp.where(take, goals[r], goal[i])
+            count = count + jnp.where(hit, 1, 0)
+        for i in range(cap):
+            slots_ref[owner * cap + i] = row[i]
+            for s in range(sec_dev):
+                marks_ref[(owner * cap + i) * sec_dev + s] = jnp.where(goal[i] == low + s, 1.0, 0.0).astype(F32)
+
     peers = cores - 1 + mpo - 1 + jnp.minimum(z, 1) + jnp.minimum(n - 1 - z, 1)
     pl.semaphore_wait(barrier, peers)
 
@@ -84,10 +104,10 @@
         t_right = jnp.where(odd, n - 1 - half, ahead + half)
         return jnp.where(near_left, t_left, t_right)
 
-    def sib_copy(t):
-        return pltpu.make_async_remote_copy(
-            src_ref=sib_send.at[t], dst_ref=sib_recv.at[t],
-            send_sem=sib_ssem.at[t], recv_sem=sib_rsem.at[t],
+    def sib_copy(t, row0, rows, i):
+        return pltpu.make_async_remote_copy(
+            src_ref=sib_send.at[t, :, row0:row0 + rows], dst_ref=sib_recv.at[t, :, row0:row0 + rows],
+            send_sem=sib_ssem.at[t, i], recv_sem=sib_rsem.at[t, i],
             device_id=sibling, device_id_type=MESH)
 
     def x_copy(t, s, d):
@@ -149,17 +169,20 @@
             send_sem=fb_ssem.at[d - 1, s], recv_sem=fb_rsem.at[o, s],
             device_id={"mpo": o}, device_id_type=MESH).wait_recv()
 
+    def add_to(ref, values):
+        total = ref[...].astype(F32)
+        for v in values:
+            total = total + v.astype(F32)
+        ref[...] = total.astype(BF16)
+
     load_psi().wait()
-    col_tile = min(cols, 256)
-
-    @pl.loop(0, terms)
-    def _(r):
-        load_right(r).wait()
-        j = lax.rem(r, sec_dev)
-        for c0 in range(0, cols, col_tile):
-            rv[r, :, c0:c0 + col_tile] = jnp.dot(
-                pv[j], rv[r, :, c0:c0 + col_tile], preferred_element_type=F32
-            ).astype(BF16)
+    @pl.loop(0, terms // sec_dev)
+    def _(w):
+        for j in range(sec_dev):
+            load_right(w * sec_dev + j).wait()
+        for j in range(sec_dev):
+            r = w * sec_dev + j
+            rv[r] = jnp.dot(pv[j], rv[r], preferred_element_type=F32).astype(BF16)
 
     @pl.loop(0, terms)
     def _(r):
@@ -177,14 +200,14 @@
                 total = term if total is None else total + term
             yield s, total.astype(BF16)
 
-    parts = [(m * hx, hx, m) for m in range(mpo)] + [(mpo * hx, hb, None)]
+    parts = [(mpo * hx, hb, None)] + [(m * hx, hx, m) for m in range(mpo)]
 
     def make_sums(t):
         if cores == 2:
-            for row0, rows, m in parts:
+            for i, (row0, rows, m) in enumerate(parts):
                 for s, value in partial_rows(t * cores + (1 - c), row0, rows):
                     sib_send[t, s, row0:row0 + rows, :] = value
-            sib_copy(t).start()
+                sib_copy(t, row0, rows, i).start()
         for row0, rows, m in parts:
             for s, value in partial_rows(t * cores + c, row0, rows):
                 if m is None:
@@ -194,74 +217,72 @@
 
     def add_sibling(t):
         if cores == 2:
-            sib_copy(t).wait_recv()
+            for i, (row0, rows, m) in enumerate(parts):
+                sib_copy(t, row0, rows, i).wait_recv()
+                for s in range(sec_dev):
+                    ref = own_b.at[t, s] if m is None else own_p.at[t, m, s]
+                    add_to(ref, [sib_recv[t, s, row0:row0 + rows, :]])
+                if m is None:
+                    send_b(t)
+        else:
+            send_b(t)
         for s in range(sec_dev):
-            if cores == 2:
-                for m in range(mpo):
-                    own_p[t, m, s] = (
-                        own_p[t, m, s].astype(F32)
-                        + sib_recv[t, s, m * hx:(m + 1) * hx, :].astype(F32)
-                    ).astype(BF16)
-                own_b[t, s] = (
-                    own_b[t, s].astype(F32) + sib_recv[t, s, mpo * hx:, :].astype(F32)
-                ).astype(BF16)
             for d in range(1, mpo):
                 x_copy(t, s, d).start()
 
-            @pl.when(z == 0)
-            def _():
-                @pl.when(t > 0)
-                def _():
-                    zb_copy(t, s, t, right_dev).start()
-
-            @pl.when(z == n - 1)
-            def _():
-                @pl.when(t < n - 1)
-                def _():
-                    zb_copy(t, s, jnp.where(t == z - 1, n, t), left_dev).start()
+    def send_b(t):
+        @pl.when(jnp.logical_and(z == 0, t > 0))
+        def _():
+            for s in range(sec_dev):
+                zb_copy(t, s, t, right_dev).start()
+
+        @pl.when(jnp.logical_and(z == n - 1, t < n - 1))
+        def _():
+            for s in range(sec_dev):
+                zb_copy(t, s, jnp.where(t == z - 1, n, t), left_dev).start()
 
     @pl.loop(0, n)
     def _(k):
         make_sums(target(k))
-
-        @pl.when(k > 0)
-        def _():
-            add_sibling(target(k - 1))
-
-    add_sibling(z)
-
-    def add_to(ref, values):
-        total = ref[...].astype(F32)
-        for v in values:
-            total = total + v.astype(F32)
-        ref[...] = total.astype(BF16)
-
-    @pl.loop(0, n - 1)
-    def _(k):
-        t = target(k)
-        inside = jnp.logical_or(jnp.logical_and(t > z, z > 0), jnp.logical_and(t < z, z < n - 1))
-
-        @pl.loop(0, sec_dev)
-        def _(s):
-            @pl.when(inside)
-            def _():
-                zb_copy(t, s, t, right_dev).wait_recv()
-                add_to(own_b.at[t, s], [z_b[t, s]])
-                z_send(zb_copy, t, s)
-
-            for d in range(1, mpo):
-                x_wait(t, s, d)
-
-            @pl.when(inside)
-            def _():
-                zp_copy(t, s, t, right_dev).wait_recv()
-                add_to(own_p.at[t, me, s], [x_recv[d, t, s] for d in range(mpo - 1)] + [z_p[t, s]])
-
-            @pl.when(jnp.logical_not(inside))
-            def _():
-                add_to(own_p.at[t, me, s], [x_recv[d, t, s] for d in range(mpo - 1)])
-
-            z_send(zp_copy, t, s)
+        add_sibling(target(k))
+
+    def pass_b(t, s, upstream):
+        @pl.when(upstream)
+        def _():
+            zb_copy(t, s, t, right_dev).wait_recv()
+            add_to(own_b.at[t, s], [z_b[t, s]])
+            z_send(zb_copy, t, s)
+
+    def pass_p(t, s, upstream):
+        for d in range(1, mpo):
+            x_wait(t, s, d)
+        over_x = [x_recv[d, t, s] for d in range(mpo - 1)]
+
+        @pl.when(upstream)
+        def _():
+            zp_copy(t, s, t, right_dev).wait_recv()
+            add_to(own_p.at[t, me, s], over_x + [z_p[t, s]])
+
+        @pl.when(jnp.logical_not(upstream))
+        def _():
+            add_to(own_p.at[t, me, s], over_x)
+
+        z_send(zp_copy, t, s)
+
+    def along_z(pass_on):
+        @pl.loop(0, n - 1)
+        def _(step):
+            @pl.loop(0, sec_dev)
+            def _(s):
+                @pl.when(step >= z)
+                def _():
+                    pass_on(n - 1 - (step - z), s, z > 0)
+
+                @pl.when(step >= n - 1 - z)
+                def _():
+                    pass_on(step - (n - 1 - z), s, z < n - 1)
+
+    along_z(pass_b)
 
     @pl.loop(0, sec_dev)
     def _(s):
@@ -278,6 +299,12 @@
         fin_b[me, s] = own_b[z, s]
         for d in range(1, mpo):
             fb_copy(s, d).start()
+
+    along_z(pass_p)
+
+    @pl.loop(0, sec_dev)
+    def _(s):
+        for d in range(1, mpo):
             x_wait(z, s, d)
         add_to(own_p.at[z, me, s], [x_recv[d, z, s] for d in range(mpo - 1)])
 
@@ -311,7 +338,8 @@
     @pl.loop(0, n)
     def _(t):
         if cores == 2:
-            sib_copy(t).wait_send()
+            for i, (row0, rows, m) in enumerate(parts):
+                sib_copy(t, row0, rows, i).wait_send()
 
         @pl.loop(0, sec_dev)
         def _(s):
@@ -340,17 +368,6 @@
     cap = max(2, -(-terms // sec_count))
     hx = first_rows(width, mpo)
     hb = width - mpo * hx
-    flat = targets.T.reshape(terms)
-    owner, within = flat // sec_dev, flat % sec_dev
-    rows = jnp.arange(terms)
-    earlier = (owner[:, None] == owner[None, :]) & (rows[None, :] < rows[:, None])
-    slot = owner * cap + jnp.sum(earlier.astype(jnp.int32), axis=1)
-    placing = jnp.arange(sec_count * cap)[:, None] == slot[None, :]
-    slots = jnp.sum(jnp.where(placing, rows[None, :], 0), axis=1).astype(jnp.int32)
-    marks = jnp.any(
-        placing[:, None, :] & (within[None, None, :] == jnp.arange(sec_dev)[None, :, None]), axis=2
-    ).astype(F32).reshape(-1)
-
     vm = lambda *shape: pltpu.VMEM(shape, BF16)
     sem = lambda *shape: pltpu.SemaphoreType.DMA(shape)
     sib = (n, sec_dev, width, cols) if cores == 2 else (1, 1, 16, 128)
@@ -358,16 +375,17 @@
     return pl.pallas_call(
         functools.partial(kernel, n, cores, mpo, cap, hx),
         out_shape=jax.ShapeDtypeStruct((sec_dev, width, cols), BF16),
-        in_specs=[pl.BlockSpec(memory_space=pltpu.SMEM)] * 2 + [pl.BlockSpec(memory_space=pl.ANY)] * 3,
+        in_specs=[pl.BlockSpec(memory_space=pltpu.SMEM)] + [pl.BlockSpec(memory_space=pl.ANY)] * 3,
         out_specs=pl.BlockSpec(memory_space=pltpu.VMEM),
         scratch_shapes=[
+            pltpu.SMEM((sec_count * cap,), jnp.int32), pltpu.SMEM((sec_count * cap * sec_dev,), F32),
             vm(sec_dev, width, width), vm(terms, width, width), vm(terms, width, cols),
             vm(*sib), vm(*sib),
             vm(n, mpo, sec_dev, hx, cols), vm(n, sec_dev, hb, cols),
             vm(xs, n, sec_dev, hx, cols),
             vm(n + 1, sec_dev, hx, cols), vm(n + 1, sec_dev, hb, cols),
             vm(mpo, sec_dev, hx, cols), vm(mpo, sec_dev, hb, cols),
-            sem(2 * terms + 1), sem(n), sem(n),
+            sem(2 * terms + 1), sem(n, mpo + 1), sem(n, mpo + 1),
             sem(xs, n, sec_dev), sem(xs, n, sec_dev),
             sem(n, sec_dev), sem(n + 1, sec_dev), sem(n, sec_dev), sem(n + 1, sec_dev),
             sem(xs, sec_dev), sem(mpo, sec_dev), sem(xs, sec_dev), sem(mpo, sec_dev),
@@ -380,7 +398,7 @@
             bytes_accessed=2 * terms * width * (width + cols), transcendentals=0,
         ),
     )(
-        slots, marks, psi, left_env.reshape(terms, width, width), right_env.reshape(terms, width, cols)
+        targets, psi, left_env.reshape(terms, width, width), right_env.reshape(terms, width, cols)
     )
 
 

time: 113 us -> 92.6 us (0.82); the launches traced: 113 us -> 91.3 us
  Pallas kernels: 107 us -> 88.6 us
  other arithmetic: 2.38 us -> 0 us
  local copies, waits for them, and re-layouts: 3.93 us -> 2.65 us
    pallas_call x1, Pallas kernels: 107 us -> 88.6 us  [local(): pl.pallas_call(functools.partial(kernel, n, cores, mpo, cap, hx), out_sha...]
where the time goes in v3:
time: 92.6 us; the launch traced here: 91.3 us
  Pallas kernels  88.6 us (96%)
  local copies, waits for them, and re-layouts  2.65 us (3%)
    pallas_call x1, Pallas kernels, local(): pl.pallas_call(functools.partial(kernel, n, cores, mpo, cap, hx), out_sha...  88.6 us
    unnamed x1, local copies, waits for them, and re-layouts  2.65 us

profile of v3, /device:TPU:0, one launch (start us, length us, event | category | flops | bytes accessed | tf_op | source)
XLA Modules:
  0.0 91.3 jit_solution(12996877826416273114)
XLA Ops:
  0.0 88.6 %shard_map.46 = bf16[3,512,512]{2,1,0:T(8,128)(2,1)} custom-call(s32[3,7]{1,0:T(4,128)} %targets_ref.1, bf16[3,512,512]{2,1,0:T(8,128)(2,1)} %psi_hbm.1, bf16[21,512,512]{2,1,0:T(8,128)(2,1)} %bitcast.2, bf16[21,512,512]{2,1,0:T(8,128)(2,1)} %bitcast.3), custom_call_target="tpu_custom_call" | custom-call | flops 11274289152 | bytes 22020096 | tf_op jit(solution)/shard_map/pallas_call | solution.py:375
  88.6 2.7 %copy.6 = bf16[3,512,512]{2,1,0:T(8,128)(2,1)} copy(bf16[3,512,512]{2,1,0:T(8,128)(2,1)} %shard_map.46) | data formatting | bytes 3145728

commit v4 on v3

--- a/solution.py
+++ b/solution.py
@@ -46,16 +46,6 @@
     def load_left(r):
         return pltpu.make_async_copy(left_hbm.at[r], lv.at[r], in_sem.at[terms + r])
 
-    load_psi().start()
-
-    @pl.loop(0, terms)
-    def _(r):
-        load_right(r).start()
-
-    @pl.loop(0, terms)
-    def _(r):
-        load_left(r).start()
-
     barrier = pltpu.get_barrier_semaphore()
     if cores == 2:
         pl.semaphore_signal(barrier, inc=1, device_id=sibling, device_id_type=MESH)
@@ -69,6 +59,16 @@
     @pl.when(z < n - 1)
     def _():
         pl.semaphore_signal(barrier, inc=1, device_id=right_dev, device_id_type=MESH)
+
+    load_psi().start()
+
+    @pl.loop(0, terms)
+    def _(r):
+        load_right(r).start()
+
+    @pl.loop(0, terms)
+    def _(r):
+        load_left(r).start()
 
     goals = [targets_ref[r % sec_dev, r // sec_dev] for r in range(terms)]
 
@@ -269,9 +269,12 @@
 
         z_send(zp_copy, t, s)
 
-    def along_z(pass_on):
+    def along_z(pass_on, between):
         @pl.loop(0, n - 1)
         def _(step):
+            if between is not None:
+                pl.when(step == min(1, n - 2))(between)
+
             @pl.loop(0, sec_dev)
             def _(s):
                 @pl.when(step >= z)
@@ -282,25 +285,25 @@
                 def _():
                     pass_on(step - (n - 1 - z), s, z < n - 1)
 
-    along_z(pass_b)
-
-    @pl.loop(0, sec_dev)
-    def _(s):
-        @pl.when(z > 0)
-        def _():
-            zb_copy(z, s, z, left_dev).wait_recv()
-            add_to(own_b.at[z, s], [z_b[z, s]])
-
-        @pl.when(z < n - 1)
-        def _():
-            zb_copy(z, s, n, right_dev).wait_recv()
-            add_to(own_b.at[z, s], [z_b[n, s]])
-
-        fin_b[me, s] = own_b[z, s]
-        for d in range(1, mpo):
-            fb_copy(s, d).start()
-
-    along_z(pass_p)
+    def own_rows_b():
+        @pl.loop(0, sec_dev)
+        def _(s):
+            @pl.when(z > 0)
+            def _():
+                zb_copy(z, s, z, left_dev).wait_recv()
+                add_to(own_b.at[z, s], [z_b[z, s]])
+
+            @pl.when(z < n - 1)
+            def _():
+                zb_copy(z, s, n, right_dev).wait_recv()
+                add_to(own_b.at[z, s], [z_b[n, s]])
+
+            fin_b[me, s] = own_b[z, s]
+            for d in range(1, mpo):
+                fb_copy(s, d).start()
+
+    along_z(pass_b, None)
+    along_z(pass_p, own_rows_b)
 
     @pl.loop(0, sec_dev)
     def _(s):

time: 92.6 us -> 92.6 us (level)
  no operation moved by 1% of the time
where the time goes in v4:
time: 92.6 us; the launch traced here: 91.4 us
  Pallas kernels  88.7 us (96%)
  local copies, waits for them, and re-layouts  2.65 us (3%)
    pallas_call x1, Pallas kernels, local(): pl.pallas_call(functools.partial(kernel, n, cores, mpo, cap, hx), out_sha...  88.7 us
    unnamed x1, local copies, waits for them, and re-layouts  2.65 us

profile of v4, /device:TPU:0, one launch (start us, length us, event | category | flops | bytes accessed | tf_op | source)
XLA Modules:
  0.0 91.4 jit_solution(17257214413485901762)
XLA Ops:
  0.0 88.7 %shard_map.46 = bf16[3,512,512]{2,1,0:T(8,128)(2,1)} custom-call(s32[3,7]{1,0:T(4,128)} %targets_ref.1, bf16[3,512,512]{2,1,0:T(8,128)(2,1)} %psi_hbm.1, bf16[21,512,512]{2,1,0:T(8,128)(2,1)} %bitcast.2, bf16[21,512,512]{2,1,0:T(8,128)(2,1)} %bitcast.3), custom_call_target="tpu_custom_call" | custom-call | flops 11274289152 | bytes 22020096 | tf_op jit(solution)/shard_map/pallas_call | solution.py:378
  88.7 2.7 %copy.6 = bf16[3,512,512]{2,1,0:T(8,128)(2,1)} copy(bf16[3,512,512]{2,1,0:T(8,128)(2,1)} %shard_map.46) | data formatting | bytes 3145728
